TPU v7x, 1024 devices: a whole 4x8x16 slice. The times are simulated.
1024 devices in a mesh: blk: 32 (over z, x_lo), grp: 32 (over x_hi, y, core).
Axes of the slice: x: 4 (x_hi: 2, x_lo: 2; x = x_hi * 2 + x_lo), y: 8, z: 16, core: 2. Of those that a mesh axis runs over, the one named last changes fastest.
Arguments:
- image_embed: bfloat16 [196608, 1152], P(('blk', 'grp')), may hold values from -0.1875 to 0.1875
- text_embed: bfloat16 [196608, 1152], P(('blk', 'grp')), may hold values from -0.1875 to 0.1875
- log_scale: float32 [1], replicated, may hold values from 2.3 to 3
- logit_bias: float32 [1], replicated, may hold values from -3 to -1
Outputs:
- image_grad: float32 [196608, 1152], P(('blk', 'grp'))
- text_grad: float32 [196608, 1152], P(('blk', 'grp'))
- row_loss: float32 [196608], P(('blk', 'grp'))
All inputs are finite; a program needn't handle non-finite values.
Results may differ from a plain program's by a relative error of at most 0.005.
Values may be sent and summed in bfloat16 or wider, within the bound.
A program may use at most 32 MiB of HBM per device.

v0:
```python
import jax
import jax.numpy as jnp
from jax import lax
from jax.sharding import PartitionSpec as P

BLK_STEPS = 2
GRP_STEPS = 4


epsilon = 1e-06


def shifted(value, axis, steps):
    count = lax.axis_size(axis)
    pairs = [(source, (source + steps) % count) for source in range(count)]
    return lax.ppermute(value, axis, pairs)


def unit_rows(embed):
    values = embed.astype(jnp.float32)
    row_norm = jnp.sqrt(jnp.sum(values * values, axis=1, keepdims=True) + epsilon)
    unit_vec = values / row_norm
    return (row_norm, unit_vec, unit_vec.astype(jnp.bfloat16))


def back_norm(unit_vec, row_norm, hat_grad):
    along = jnp.sum(unit_vec * hat_grad, axis=1, keepdims=True)
    return (hat_grad - unit_vec * along) / row_norm


def body(image_embed, text_embed, log_scale, logit_bias):
    image_norm, image_unit, image_hat = unit_rows(image_embed)
    text_norm, text_unit, text_hat = unit_rows(text_embed)
    factor = jnp.exp(log_scale[0])
    offset_b = logit_bias[0]
    row_count = image_hat.shape[0]
    width_d = image_hat.shape[1]
    diag_sign = jnp.where(jnp.eye(row_count, dtype=bool), 1.0, -1.0).astype(jnp.float32)
    loss_total = jnp.zeros((row_count,), jnp.float32)
    grad_total = jnp.zeros((row_count, width_d), jnp.float32)
    text_total = jnp.zeros((row_count, width_d), jnp.float32)
    start_block = text_hat
    for blk_index in range(BLK_STEPS):
        if blk_index > 0:
            start_block = shifted(start_block, "blk", 1)
        text_block = start_block
        row_sum = jnp.zeros((row_count, width_d), jnp.float32)
        for grp_index in range(GRP_STEPS):
            if grp_index > 0:
                text_block = shifted(text_block, "grp", 1)
            inner_dot = lax.dot_general(
                image_hat, text_block, (((1,), (1,)), ((), ())), preferred_element_type=jnp.float32
            )
            logits = factor * inner_dot + offset_b
            sign_mat = diag_sign if blk_index == 0 and grp_index == 0 else jnp.float32(-1.0)
            margin = sign_mat * logits
            loss_total = loss_total + jnp.sum(jax.nn.softplus(-margin), axis=1)
            slope_w = (factor * -sign_mat * jax.nn.sigmoid(-margin)).astype(jnp.bfloat16)
            grad_total = grad_total + jnp.dot(
                slope_w, text_block, preferred_element_type=jnp.float32
            )
            share = lax.dot_general(
                slope_w, image_hat, (((0,), (0,)), ((), ())), preferred_element_type=jnp.float32
            )
            if grp_index == 0:
                row_sum = share
            else:
                row_sum = row_sum + shifted(share, "grp", -grp_index)
        if blk_index > 0:
            row_sum = shifted(row_sum.astype(jnp.bfloat16), "blk", -blk_index).astype(row_sum.dtype)
        text_total = text_total + row_sum
    image_grad = back_norm(image_unit, image_norm, grad_total)
    text_grad = back_norm(text_unit, text_norm, text_total)
    row_loss = loss_total / (BLK_STEPS * GRP_STEPS * row_count)
    return (image_grad, text_grad, row_loss)


def solution(mesh):
    in_specs = (P(("blk", "grp"), None), P(("blk", "grp"), None), P(), P())
    out_specs = (P(("blk", "grp"), None), P(("blk", "grp"), None), P(("blk", "grp")))
    return jax.shard_map(body, mesh=mesh, in_specs=in_specs, out_specs=out_specs, check_vma=False)
```

profile of v0, /device:TPU:1, one launch (start us, length us, event | category | flops | bytes accessed | tf_op | source)
XLA Modules:
  0.0 163.8 jit_solution(16159452284074601737)
XLA Ops:
  0.6 1.2 fusion.24
  2.1 3.9 %collective-permute-start.3 = (bf16[192,1152]{1,0:T(8,128)(2,1)S(1)}, bf16[192,1152]{1,0:T(8,128)(2,1)S(1)}, u32[]{:S(2)}, u32[]{:S(2)}) collective-permute-start(bf16[192,1152]{1,0:T(8,128)(2,1)S(1)} %fusion.44), channel_id=1, source_target_pairs={{0,32},{32,64},{64,96},{96,128},{128,160},{160,192},{192,224},{224... | collective-permute-start | bytes 1327112 | tf_op jit(solution)/shard_map/ppermute | solution.py:16
  6.0 4.0 %collective-permute-start = (bf16[192,1152]{1,0:T(8,128)(2,1)S(1)}, bf16[192,1152]{1,0:T(8,128)(2,1)S(1)}, u32[]{:S(2)}, u32[]{:S(2)}) collective-permute-start(bf16[192,1152]{1,0:T(8,128)(2,1)S(1)} %fusion.44), channel_id=1, source_target_pairs={{0,1},{1,2},{2,3},{3,4},{4,5},{5,6},{6,7},{7,8},{8,9},{9,10},{10,1... | collective-permute-start | bytes 1327112 | tf_op jit(solution)/shard_map/ppermute | solution.py:16
  11.8 0.5 fusion.28
  12.6 8.7 %collective-permute-done = bf16[192,1152]{1,0:T(8,128)(2,1)S(1)} collective-permute-done((bf16[192,1152]{1,0:T(8,128)(2,1)S(1)}, bf16[192,1152]{1,0:T(8,128)(2,1)S(1)}, u32[]{:S(2)}, u32[]{:S(2)}) %collective-permute-start) | collective-permute-done | bytes 442400 | tf_op jit(solution)/shard_map/ppermute | solution.py:16
  22.1 12.0 %collective-permute-start.7 = (f32[192,1152]{1,0:T(8,128)S(1)}, f32[192,1152]{1,0:T(8,128)S(1)}, u32[]{:S(2)}, u32[]{:S(2)}) collective-permute-start(f32[192,1152]{1,0:T(8,128)S(1)} %fusion.36), channel_id=1, source_target_pairs={{0,31},{1,0},{2,1},{3,2},{4,3},{5,4},{6,5},{7,6},{8,7},{9,8},{10,9... | collective-permute-start | bytes 2654216 | tf_op jit(solution)/shard_map/ppermute | solution.py:16
  34.1 1.9 %collective-permute-start.1 = (bf16[192,1152]{1,0:T(8,128)(2,1)S(1)}, bf16[192,1152]{1,0:T(8,128)(2,1)S(1)}, u32[]{:S(2)}, u32[]{:S(2)}) collective-permute-start(bf16[192,1152]{1,0:T(8,128)(2,1)S(1)} %collective-permute-done), channel_id=1, source_target_pairs={{0,1},{1,2},{2,3},{3,4},{4,5},{5,6},{6,7},{7,8},{8,9},{9,10},{10,1... | collective-permute-start | bytes 1327112 | tf_op jit(solution)/shard_map/ppermute | solution.py:16
  36.0 1.9 %collective-permute-start.4 = (bf16[192,1152]{1,0:T(8,128)(2,1)S(1)}, bf16[192,1152]{1,0:T(8,128)(2,1)S(1)}, u32[]{:S(2)}, u32[]{:S(2)}) collective-permute-start(bf16[192,1152]{1,0:T(8,128)(2,1)S(1)} %collective-permute-done.3), channel_id=1, source_target_pairs={{0,1},{1,2},{2,3},{3,4},{4,5},{5,6},{6,7},{7,8},{8,9},{9,10},{10,1... | collective-permute-start | bytes 1327112 | tf_op jit(solution)/shard_map/ppermute | solution.py:16
  37.9 0.5 fusion.32
  39.1 6.9 %collective-permute-done.4 = bf16[192,1152]{1,0:T(8,128)(2,1)S(1)} collective-permute-done((bf16[192,1152]{1,0:T(8,128)(2,1)S(1)}, bf16[192,1152]{1,0:T(8,128)(2,1)S(1)}, u32[]{:S(2)}, u32[]{:S(2)}) %collective-permute-start.4) | collective-permute-done | bytes 442400 | tf_op jit(solution)/shard_map/ppermute | solution.py:16
  46.0 0.4 fusion.33
  46.7 8.0 %collective-permute-start.10 = (f32[192,1152]{1,0:T(8,128)S(1)}, f32[192,1152]{1,0:T(8,128)S(1)}, u32[]{:S(2)}, u32[]{:S(2)}) collective-permute-start(f32[192,1152]{1,0:T(8,128)S(1)} %fusion.40), channel_id=1, source_target_pairs={{0,31},{1,0},{2,1},{3,2},{4,3},{5,4},{6,5},{7,6},{8,7},{9,8},{10,9... | collective-permute-start | bytes 2654216 | tf_op jit(solution)/shard_map/ppermute | solution.py:16
  54.7 1.9 %collective-permute-start.5 = (bf16[192,1152]{1,0:T(8,128)(2,1)S(1)}, bf16[192,1152]{1,0:T(8,128)(2,1)S(1)}, u32[]{:S(2)}, u32[]{:S(2)}) collective-permute-start(bf16[192,1152]{1,0:T(8,128)(2,1)S(1)} %collective-permute-done.4), channel_id=1, source_target_pairs={{0,1},{1,2},{2,3},{3,4},{4,5},{5,6},{6,7},{7,8},{8,9},{9,10},{10,1... | collective-permute-start | bytes 1327112 | tf_op jit(solution)/shard_map/ppermute | solution.py:16
  56.7 0.4 fusion.30
  57.4 6.9 %collective-permute-start.8 = (f32[192,1152]{1,0:T(8,128)S(1)}, f32[192,1152]{1,0:T(8,128)S(1)}, u32[]{:S(2)}, u32[]{:S(2)}) collective-permute-start(f32[192,1152]{1,0:T(8,128)S(1)} %fusion.37), channel_id=1, source_target_pairs={{0,30},{1,31},{2,0},{3,1},{4,2},{5,3},{6,4},{7,5},{8,6},{9,7},{10,... | collective-permute-start | bytes 2654216 | tf_op jit(solution)/shard_map/ppermute | solution.py:16
  64.3 1.9 %collective-permute-start.2 = (bf16[192,1152]{1,0:T(8,128)(2,1)S(1)}, bf16[192,1152]{1,0:T(8,128)(2,1)S(1)}, u32[]{:S(2)}, u32[]{:S(2)}) collective-permute-start(bf16[192,1152]{1,0:T(8,128)(2,1)S(1)} %collective-permute-done.1), channel_id=1, source_target_pairs={{0,1},{1,2},{2,3},{3,4},{4,5},{5,6},{6,7},{7,8},{8,9},{9,10},{10,1... | collective-permute-start | bytes 1327112 | tf_op jit(solution)/shard_map/ppermute | solution.py:16
  67.3 5.1 %collective-permute-start.11 = (f32[192,1152]{1,0:T(8,128)S(1)}, f32[192,1152]{1,0:T(8,128)S(1)}, u32[]{:S(2)}, u32[]{:S(2)}) collective-permute-start(f32[192,1152]{1,0:T(8,128)S(1)} %fusion.41), channel_id=1, source_target_pairs={{0,30},{1,31},{2,0},{3,1},{4,2},{5,3},{6,4},{7,5},{8,6},{9,7},{10,... | collective-permute-start | bytes 2654216 | tf_op jit(solution)/shard_map/ppermute | solution.py:16
  72.5 3.4 %collective-permute-start.6 = (bf16[192,1152]{1,0:T(8,128)(2,1)S(1)}, bf16[192,1152]{1,0:T(8,128)(2,1)S(1)}, u32[]{:S(2)}, u32[]{:S(2)}) collective-permute-start(bf16[192,1152]{1,0:T(8,128)(2,1)S(1)} %collective-permute-done.5), channel_id=1, source_target_pairs={{0,1},{1,2},{2,3},{3,4},{4,5},{5,6},{6,7},{7,8},{8,9},{9,10},{10,1... | collective-permute-start | bytes 1327112 | tf_op jit(solution)/shard_map/ppermute | solution.py:16
  75.8 0.4 fusion.31
  77.0 4.1 %collective-permute-done.6 = bf16[192,1152]{1,0:T(8,128)(2,1)S(1)} collective-permute-done((bf16[192,1152]{1,0:T(8,128)(2,1)S(1)}, bf16[192,1152]{1,0:T(8,128)(2,1)S(1)}, u32[]{:S(2)}, u32[]{:S(2)}) %collective-permute-start.6) | collective-permute-done | bytes 442400 | tf_op jit(solution)/shard_map/ppermute | solution.py:16
  81.1 0.4 fusion.35
  81.8 2.2 %collective-permute-start.12 = (f32[192,1152]{1,0:T(8,128)S(1)}, f32[192,1152]{1,0:T(8,128)S(1)}, u32[]{:S(2)}, u32[]{:S(2)}) collective-permute-start(f32[192,1152]{1,0:T(8,128)S(1)} %fusion.42), channel_id=1, source_target_pairs={{0,29},{1,30},{2,31},{3,0},{4,1},{5,2},{6,3},{7,4},{8,5},{9,6},{10... | collective-permute-start | bytes 2654216 | tf_op jit(solution)/shard_map/ppermute | solution.py:16
  84.7 0.5 multiply_reduce_fusion.1
  85.2 1.9 %collective-permute-start.9 = (f32[192,1152]{1,0:T(8,128)S(1)}, f32[192,1152]{1,0:T(8,128)S(1)}, u32[]{:S(2)}, u32[]{:S(2)}) collective-permute-start(f32[192,1152]{1,0:T(8,128)S(1)} %fusion.38), channel_id=1, source_target_pairs={{0,29},{1,30},{2,31},{3,0},{4,1},{5,2},{6,3},{7,4},{8,5},{9,6},{10... | collective-permute-start | bytes 2654216 | tf_op jit(solution)/shard_map/ppermute | solution.py:16
  87.1 0.6 add_multiply_fusion
  87.7 15.3 %collective-permute-done.11 = f32[192,1152]{1,0:T(8,128)S(1)} collective-permute-done((f32[192,1152]{1,0:T(8,128)S(1)}, f32[192,1152]{1,0:T(8,128)S(1)}, u32[]{:S(2)}, u32[]{:S(2)}) %collective-permute-start.11) | collective-permute-done | bytes 884768 | tf_op jit(solution)/shard_map/ppermute | solution.py:16
  103.0 28.6 %collective-permute-done.12 = f32[192,1152]{1,0:T(8,128)S(1)} collective-permute-done((f32[192,1152]{1,0:T(8,128)S(1)}, f32[192,1152]{1,0:T(8,128)S(1)}, u32[]{:S(2)}, u32[]{:S(2)}) %collective-permute-start.12) | collective-permute-done | bytes 884768 | tf_op jit(solution)/shard_map/ppermute | solution.py:16
  131.9 10.1 %collective-permute-start.13 = (bf16[192,1152]{1,0:T(8,128)(2,1)S(1)}, bf16[192,1152]{1,0:T(8,128)(2,1)S(1)}, u32[]{:S(2)}, u32[]{:S(2)}) collective-permute-start(bf16[192,1152]{1,0:T(8,128)(2,1)S(1)} %fusion.6), channel_id=1, source_target_pairs={{0,992},{32,0},{64,32},{96,64},{128,96},{160,128},{192,160},{224,1... | collective-permute-start | bytes 1327112 | tf_op jit(solution)/shard_map/ppermute | solution.py:16
  142.0 1.1 subtract_divide_fusion.1
  143.1 19.0 %collective-permute-done.9 = f32[192,1152]{1,0:T(8,128)S(1)} collective-permute-done((f32[192,1152]{1,0:T(8,128)S(1)}, f32[192,1152]{1,0:T(8,128)S(1)}, u32[]{:S(2)}, u32[]{:S(2)}) %collective-permute-start.9) | collective-permute-done | bytes 884768 | tf_op jit(solution)/shard_map/ppermute | solution.py:16
  162.1 0.6 multiply_reduce_fusion
  162.7 1.1 subtract_divide_fusion
  (33 shorter events, 6.0 us)
Async XLA Ops:
  0.6 1.3 copy-start.1
  1.9 8.2 %copy-start = (bf16[192,1152]{1,0:T(8,128)(2,1)S(1)}, bf16[192,1152]{1,0:T(8,128)(2,1)}, u32[]{:S(2)}) copy-start(bf16[192,1152]{1,0:T(8,128)(2,1)} %param.4) | copy-start | bytes 1327108
  2.1 33.9 %collective-permute-start.3 = (bf16[192,1152]{1,0:T(8,128)(2,1)S(1)}, bf16[192,1152]{1,0:T(8,128)(2,1)S(1)}, u32[]{:S(2)}, u32[]{:S(2)}) collective-permute-start(bf16[192,1152]{1,0:T(8,128)(2,1)S(1)} %fusion.44), channel_id=1, source_target_pairs={{0,32},{32,64},{64,96},{96,128},{128,160},{160,192},{192,224},{224... | collective-permute-start | bytes 1327112 | tf_op jit(solution)/shard_map/ppermute | solution.py:16
  6.0 15.3 %collective-permute-start = (bf16[192,1152]{1,0:T(8,128)(2,1)S(1)}, bf16[192,1152]{1,0:T(8,128)(2,1)S(1)}, u32[]{:S(2)}, u32[]{:S(2)}) collective-permute-start(bf16[192,1152]{1,0:T(8,128)(2,1)S(1)} %fusion.44), channel_id=1, source_target_pairs={{0,1},{1,2},{2,3},{3,4},{4,5},{5,6},{6,7},{7,8},{8,9},{9,10},{10,1... | collective-permute-start | bytes 1327112 | tf_op jit(solution)/shard_map/ppermute | solution.py:16
  22.1 121.0 %collective-permute-start.7 = (f32[192,1152]{1,0:T(8,128)S(1)}, f32[192,1152]{1,0:T(8,128)S(1)}, u32[]{:S(2)}, u32[]{:S(2)}) collective-permute-start(f32[192,1152]{1,0:T(8,128)S(1)} %fusion.36), channel_id=1, source_target_pairs={{0,31},{1,0},{2,1},{3,2},{4,3},{5,4},{6,5},{7,6},{8,7},{9,8},{10,9... | collective-permute-start | bytes 2654216 | tf_op jit(solution)/shard_map/ppermute | solution.py:16
  34.1 22.6 %collective-permute-start.1 = (bf16[192,1152]{1,0:T(8,128)(2,1)S(1)}, bf16[192,1152]{1,0:T(8,128)(2,1)S(1)}, u32[]{:S(2)}, u32[]{:S(2)}) collective-permute-start(bf16[192,1152]{1,0:T(8,128)(2,1)S(1)} %collective-permute-done), channel_id=1, source_target_pairs={{0,1},{1,2},{2,3},{3,4},{4,5},{5,6},{6,7},{7,8},{8,9},{9,10},{10,1... | collective-permute-start | bytes 1327112 | tf_op jit(solution)/shard_map/ppermute | solution.py:16
  36.0 10.0 %collective-permute-start.4 = (bf16[192,1152]{1,0:T(8,128)(2,1)S(1)}, bf16[192,1152]{1,0:T(8,128)(2,1)S(1)}, u32[]{:S(2)}, u32[]{:S(2)}) collective-permute-start(bf16[192,1152]{1,0:T(8,128)(2,1)S(1)} %collective-permute-done.3), channel_id=1, source_target_pairs={{0,1},{1,2},{2,3},{3,4},{4,5},{5,6},{6,7},{7,8},{8,9},{9,10},{10,1... | collective-permute-start | bytes 1327112 | tf_op jit(solution)/shard_map/ppermute | solution.py:16
  46.7 38.5 %collective-permute-start.10 = (f32[192,1152]{1,0:T(8,128)S(1)}, f32[192,1152]{1,0:T(8,128)S(1)}, u32[]{:S(2)}, u32[]{:S(2)}) collective-permute-start(f32[192,1152]{1,0:T(8,128)S(1)} %fusion.40), channel_id=1, source_target_pairs={{0,31},{1,0},{2,1},{3,2},{4,3},{5,4},{6,5},{7,6},{8,7},{9,8},{10,9... | collective-permute-start | bytes 2654216 | tf_op jit(solution)/shard_map/ppermute | solution.py:16
  54.7 11.9 %collective-permute-start.5 = (bf16[192,1152]{1,0:T(8,128)(2,1)S(1)}, bf16[192,1152]{1,0:T(8,128)(2,1)S(1)}, u32[]{:S(2)}, u32[]{:S(2)}) collective-permute-start(bf16[192,1152]{1,0:T(8,128)(2,1)S(1)} %collective-permute-done.4), channel_id=1, source_target_pairs={{0,1},{1,2},{2,3},{3,4},{4,5},{5,6},{6,7},{7,8},{8,9},{9,10},{10,1... | collective-permute-start | bytes 1327112 | tf_op jit(solution)/shard_map/ppermute | solution.py:16
  57.4 85.7 %collective-permute-start.8 = (f32[192,1152]{1,0:T(8,128)S(1)}, f32[192,1152]{1,0:T(8,128)S(1)}, u32[]{:S(2)}, u32[]{:S(2)}) collective-permute-start(f32[192,1152]{1,0:T(8,128)S(1)} %fusion.37), channel_id=1, source_target_pairs={{0,30},{1,31},{2,0},{3,1},{4,2},{5,3},{6,4},{7,5},{8,6},{9,7},{10,... | collective-permute-start | bytes 2654216 | tf_op jit(solution)/shard_map/ppermute | solution.py:16
  64.3 8.2 %collective-permute-start.2 = (bf16[192,1152]{1,0:T(8,128)(2,1)S(1)}, bf16[192,1152]{1,0:T(8,128)(2,1)S(1)}, u32[]{:S(2)}, u32[]{:S(2)}) collective-permute-start(bf16[192,1152]{1,0:T(8,128)(2,1)S(1)} %collective-permute-done.1), channel_id=1, source_target_pairs={{0,1},{1,2},{2,3},{3,4},{4,5},{5,6},{6,7},{7,8},{8,9},{9,10},{10,1... | collective-permute-start | bytes 1327112 | tf_op jit(solution)/shard_map/ppermute | solution.py:16
  67.3 35.7 %collective-permute-start.11 = (f32[192,1152]{1,0:T(8,128)S(1)}, f32[192,1152]{1,0:T(8,128)S(1)}, u32[]{:S(2)}, u32[]{:S(2)}) collective-permute-start(f32[192,1152]{1,0:T(8,128)S(1)} %fusion.41), channel_id=1, source_target_pairs={{0,30},{1,31},{2,0},{3,1},{4,2},{5,3},{6,4},{7,5},{8,6},{9,7},{10,... | collective-permute-start | bytes 2654216 | tf_op jit(solution)/shard_map/ppermute | solution.py:16
  72.5 8.6 %collective-permute-start.6 = (bf16[192,1152]{1,0:T(8,128)(2,1)S(1)}, bf16[192,1152]{1,0:T(8,128)(2,1)S(1)}, u32[]{:S(2)}, u32[]{:S(2)}) collective-permute-start(bf16[192,1152]{1,0:T(8,128)(2,1)S(1)} %collective-permute-done.5), channel_id=1, source_target_pairs={{0,1},{1,2},{2,3},{3,4},{4,5},{5,6},{6,7},{7,8},{8,9},{9,10},{10,1... | collective-permute-start | bytes 1327112 | tf_op jit(solution)/shard_map/ppermute | solution.py:16
  81.8 49.8 %collective-permute-start.12 = (f32[192,1152]{1,0:T(8,128)S(1)}, f32[192,1152]{1,0:T(8,128)S(1)}, u32[]{:S(2)}, u32[]{:S(2)}) collective-permute-start(f32[192,1152]{1,0:T(8,128)S(1)} %fusion.42), channel_id=1, source_target_pairs={{0,29},{1,30},{2,31},{3,0},{4,1},{5,2},{6,3},{7,4},{8,5},{9,6},{10... | collective-permute-start | bytes 2654216 | tf_op jit(solution)/shard_map/ppermute | solution.py:16
  85.2 76.9 %collective-permute-start.9 = (f32[192,1152]{1,0:T(8,128)S(1)}, f32[192,1152]{1,0:T(8,128)S(1)}, u32[]{:S(2)}, u32[]{:S(2)}) collective-permute-start(f32[192,1152]{1,0:T(8,128)S(1)} %fusion.38), channel_id=1, source_target_pairs={{0,29},{1,30},{2,31},{3,0},{4,1},{5,2},{6,3},{7,4},{8,5},{9,6},{10... | collective-permute-start | bytes 2654216 | tf_op jit(solution)/shard_map/ppermute | solution.py:16
  131.9 30.2 %collective-permute-start.13 = (bf16[192,1152]{1,0:T(8,128)(2,1)S(1)}, bf16[192,1152]{1,0:T(8,128)(2,1)S(1)}, u32[]{:S(2)}, u32[]{:S(2)}) collective-permute-start(bf16[192,1152]{1,0:T(8,128)(2,1)S(1)} %fusion.6), channel_id=1, source_target_pairs={{0,992},{32,0},{64,32},{96,64},{128,96},{160,128},{192,160},{224,1... | collective-permute-start | bytes 1327112 | tf_op jit(solution)/shard_map/ppermute | solution.py:16
where the time goes:
time: 164 us
  waiting for transfers between devices  82.5 us (50%)
  starting transfers between devices  65.2 us (40%)
  matrix products  9.19 us (6%)
  other arithmetic  4.6 us (3%)
  between operations  2.25 us (1%)
    ppermute x14, waiting for transfers between devices, shifted(): return lax.ppermute(value, axis, pairs)  82.5 us
    ppermute x14, starting transfers between devices, shifted(): return lax.ppermute(value, axis, pairs)  65.2 us
    dot_general x8, matrix products, body(): lax.dot_general(image_hat, text_block, (((1,), (1,)), ((), ())), preferre...  3.58 us
  transfers between devices with their start and end apart: 14, of which 6 were waited for; matrix products, arithmetic and copies ran while one was open for 7% of the time, Pallas kernels for 0%

commit v1 on v0

v1 whole, which is shorter than its diff:
```python
import functools

import jax
import jax.numpy as jnp
from jax import lax
from jax.experimental import pallas as pl
from jax.experimental.pallas import tpu as pltpu
from jax.sharding import PartitionSpec as P

MESH = pl.DeviceIdType.MESH
EPS = 1e-06
PAIRS = 8
T1, T2, T3, IM, PA, PB, QS, GS = range(8)


def kernel(n_blk, n_grp, nc, img_ref, txt_ref, scale_ref, bias_ref, ig_ref, tg_ref, loss_ref,
           xs, tb, gi, pt, ra, rb, rq, rgi, s1, s3, sq, sgi, inorm, tnorm, la, ls, lr,
           send_sem, recv_sem, lsend, lrecv):
    blk, grp = lax.axis_index("blk"), lax.axis_index("grp")
    core = lax.rem(grp, 2)
    rows, width = img_ref.shape
    ch = rows // nc
    part = width // 3

    def to(db, dg):
        return (lax.rem(blk + db + n_blk, n_blk), lax.rem(grp + dg + n_grp, n_grp))

    def copy(stream, c, src, dst, target):
        r = pl.ds(c * ch, ch)
        return pltpu.make_async_remote_copy(
            src_ref=src.at[r], dst_ref=dst.at[r],
            send_sem=send_sem.at[stream, c], recv_sem=recv_sem.at[stream, c],
            device_id=target, device_id_type=MESH)

    def got(stream, c, dst):
        copy(stream, c, dst, dst, to(0, 1)).wait_recv()

    def sent(stream, c, src):
        copy(stream, c, src, src, to(0, 1)).wait_send()

    def each(fn):
        for c in range(nc):
            fn(c)

    barrier = pltpu.get_barrier_semaphore()
    for db, dg in ((0, 1), (0, -1), (0, 2), (0, -2), (1, 0), (-1, 0)):
        pl.semaphore_signal(barrier, inc=1, device_id=to(db, dg), device_id_type=MESH)

    def normalize(src, norm, dst):
        def chunk(c, _):
            r = pl.ds(pl.multiple_of(c * 32, 32), 32)
            v = src[r, :].astype(jnp.float32)
            n = jnp.sqrt(jnp.sum(v * v, axis=1, keepdims=True) + EPS)
            norm[r, :] = n
            dst[r, :] = (v / n).astype(jnp.bfloat16)
            return _
        lax.fori_loop(0, rows // 32, chunk, 0)

    normalize(txt_ref, tnorm, tb.at[0])
    normalize(img_ref, inorm, xs.at[0])
    gi[...] = jnp.zeros_like(gi)
    pt[...] = jnp.zeros_like(pt)
    la[...] = jnp.zeros_like(la)
    pl.semaphore_wait(barrier, 6)

    each(lambda c: copy(T2, c, tb.at[0], tb.at[2], to(0, 2)).start())
    each(lambda c: copy(IM, c, xs.at[0], xs.at[1], to(-1, 0)).start())

    @pl.when(core == 0)
    def _():
        each(lambda c: copy(T1, c, tb.at[0], tb.at[1], to(0, 1)).start())

    factor = jnp.exp(jnp.full((1, rows), scale_ref[0], jnp.float32))
    bias = bias_ref[0]

    def compute(which, slot):
        logit = lax.dot_general(tb[slot], xs[which], (((1,), (1,)), ((), ())),
                                preferred_element_type=jnp.float32)
        logit = factor * logit + bias
        own = jnp.logical_and(which == 0, slot == 0)
        at = lax.broadcasted_iota(jnp.int32, (rows, rows), 0)
        to_ = lax.broadcasted_iota(jnp.int32, (rows, rows), 1)
        minus = jnp.where(jnp.logical_and(at == to_, own), -1.0, 1.0).astype(jnp.float32)
        x = minus * logit
        e = jnp.exp(-jnp.abs(x))
        la[which, 0:1, :] += jnp.sum(jnp.maximum(x, 0.0) + jnp.log1p(e), axis=0, keepdims=True)
        slope = (factor * minus * (jnp.where(x >= 0, 1.0, e) / (1.0 + e))).astype(jnp.bfloat16)
        for n in range(3):
            cols = slice(n * part, (n + 1) * part)
            gi[which, :, cols] += lax.dot_general(slope, tb[slot, :, cols], (((0,), (0,)), ((), ())),
                                                  preferred_element_type=jnp.float32)
            pt[slot, :, cols] += jnp.dot(slope, xs[which, :, cols], preferred_element_type=jnp.float32)

    def emit(slot, buf, stream, dst, target):
        for c in range(nc):
            r = pl.ds(c * ch, ch)
            buf[r, :] = pt[slot, r, :].astype(jnp.bfloat16)
            copy(stream, c, buf, dst, target).start()

    def pick(j, values):
        out = jnp.int32(values[-1])
        for i in range(len(values) - 1):
            out = jnp.where(j == i, values[i], out)
        return out

    def step(j, carry):
        c0, c1 = core == 0, core == 1
        at = lambda i0, i1: jnp.logical_or(jnp.logical_and(c0, j == i0), jnp.logical_and(c1, j == i1))

        @pl.when(at(1, 2))
        def _():
            for c in range(nc):
                got(T2, c, tb.at[2])
                copy(T3, c, tb.at[2], tb.at[3], to(0, 1)).start()

                @pl.when(c1)
                def _():
                    copy(T1, c, tb.at[2], tb.at[1], to(0, -1)).start()

        @pl.when(at(2, 1))
        def _():
            each(lambda c: got(T1, c, tb.at[1]))

        @pl.when(at(5, 3))
        def _():
            each(lambda c: got(T3, c, tb.at[3]))

        @pl.when(at(3, 4))
        def _():
            each(lambda c: got(IM, c, xs.at[1]))

        which = jnp.where(c0, pick(j, (0, 0, 0, 1, 1, 0, 1, 1)), pick(j, (0, 0, 0, 0, 1, 1, 1, 1)))
        slot = jnp.where(c0, pick(j, (0, 2, 1, 2, 1, 3, 3, 0)), pick(j, (0, 1, 2, 3, 3, 2, 1, 0)))
        compute(which, slot)

        @pl.when(jnp.logical_and(c0, j == 3))
        def _():
            for c in range(nc):
                r = pl.ds(c * ch, ch)
                got(PB, c, rb)
                sq[r, :] = (pt[2, r, :] + rb[r, :].astype(jnp.float32)).astype(jnp.bfloat16)
                copy(QS, c, sq, rq, to(0, -2)).start()

        @pl.when(jnp.logical_and(c0, j == 4))
        def _():
            emit(1, s1, PB, rb, to(0, 1))

        @pl.when(jnp.logical_and(c0, j == 6))
        def _():
            emit(3, s3, PA, ra, to(0, -1))

        @pl.when(jnp.logical_and(c1, j == 4))
        def _():
            emit(3, s3, PB, rb, to(0, -1))

        @pl.when(jnp.logical_and(c1, j == 6))
        def _():
            emit(1, s1, PA, ra, to(0, -1))
        return carry

    lax.fori_loop(0, 8, step, 0)

    for c in range(nc):
        r = pl.ds(c * ch, ch)
        sgi[r, :] = gi[1, r, :].astype(jnp.bfloat16)
        copy(GS, c, sgi, rgi, to(1, 0)).start()
    ls[...] = la[1]
    lcopy = pltpu.make_async_remote_copy(src_ref=ls, dst_ref=lr, send_sem=lsend, recv_sem=lrecv,
                                         device_id=to(1, 0), device_id_type=MESH)
    lcopy.start()

    @pl.when(core == 1)
    def _():
        for c in range(nc):
            r = pl.ds(c * ch, ch)
            got(PB, c, rb)
            got(PA, c, ra)
            sq[r, :] = (pt[2, r, :] + rb[r, :].astype(jnp.float32)
                        + ra[r, :].astype(jnp.float32)).astype(jnp.bfloat16)
            copy(QS, c, sq, rq, to(0, -2)).start()

    @pl.when(core == 0)
    def _():
        for c in range(nc):
            r = pl.ds(c * ch, ch)
            got(PA, c, ra)
            pt[0, r, :] += ra[r, :].astype(jnp.float32)

    def back(c, src, norm, hat, out):
        r = pl.ds(c * ch, ch)
        n = norm[r, :]
        unit = src[r, :].astype(jnp.float32) / n
        along = jnp.sum(unit * hat, axis=1, keepdims=True)
        out[r, :] = (hat - unit * along) / n

    for c in range(nc):
        r = pl.ds(c * ch, ch)
        got(GS, c, rgi)
        back(c, img_ref, inorm, gi[0, r, :] + rgi[r, :].astype(jnp.float32), ig_ref)
    lcopy.wait()
    loss_ref[...] = (la[0, 0:1, :] + lr[0:1, :]) / (PAIRS * rows)
    for c in range(nc):
        r = pl.ds(c * ch, ch)
        got(QS, c, rq)
        back(c, txt_ref, tnorm, pt[0, r, :] + rq[r, :].astype(jnp.float32), tg_ref)

    for c in range(nc):
        sent(T1, c, tb.at[1])
        sent(T2, c, tb.at[0])
        sent(T3, c, tb.at[2])
        sent(IM, c, xs.at[0])
        sent(PA, c, s1)
        sent(PB, c, s3)
        sent(QS, c, sq)
        sent(GS, c, sgi)


def solution(mesh):
    n_blk, n_grp = mesh.shape["blk"], mesh.shape["grp"]

    def body(image_embed, text_embed, log_scale, logit_bias):
        rows, width = image_embed.shape
        nc = 2
        half = lambda *shape: pltpu.VMEM(shape, jnp.bfloat16)
        full = lambda *shape: pltpu.VMEM(shape, jnp.float32)
        dma = pltpu.SemaphoreType.DMA
        vmem = pl.BlockSpec(memory_space=pltpu.VMEM)
        smem = pl.BlockSpec(memory_space=pltpu.SMEM)
        out = lambda *shape: jax.ShapeDtypeStruct(shape, jnp.float32)
        image_grad, text_grad, loss = pl.pallas_call(
            functools.partial(kernel, n_blk, n_grp, nc),
            out_shape=(out(rows, width), out(rows, width), out(1, rows)),
            in_specs=[vmem, vmem, smem, smem],
            out_specs=(vmem, vmem, vmem),
            scratch_shapes=[
                half(2, rows, width), half(4, rows, width), full(2, rows, width), full(4, rows, width),
                half(rows, width), half(rows, width), half(rows, width), half(rows, width),
                half(rows, width), half(rows, width), half(rows, width), half(rows, width),
                full(rows, 1), full(rows, 1), full(2, 8, rows), full(8, rows), full(8, rows),
                dma((8, nc)), dma((8, nc)), dma, dma,
            ],
            compiler_params=pltpu.CompilerParams(
                collective_id=0, has_side_effects=True, vmem_limit_bytes=40 << 20),
            cost_estimate=pl.CostEstimate(flops=48 * rows * rows * width, bytes_accessed=12 * rows * width,
                                          transcendentals=24 * rows * rows),
            name="band_loss",
        )(image_embed, text_embed, log_scale, logit_bias)
        return image_grad, text_grad, loss.reshape(rows)

    in_specs = (P(("blk", "grp"), None), P(("blk", "grp"), None), P(), P())
    out_specs = (P(("blk", "grp"), None), P(("blk", "grp"), None), P(("blk", "grp")))
    return jax.shard_map(body, mesh=mesh, in_specs=in_specs, out_specs=out_specs, check_vma=False)
```

time: 164 us -> 70.8 us (0.43)
  the two profiles are of different devices: /device:TPU:1 before, /device:TPU:58 now
where the time goes in v1:
time: 70.8 us; the launch traced here: 70.6 us
  Pallas kernels  64.2 us (91%)
  local copies, waits for them, and re-layouts  4.41 us (6%)
  between operations  1.94 us (3%)
    pallas_call x1, Pallas kernels, body(): pl.pallas_call(functools.partial(kernel, n_blk, n_grp, nc), out_shape=(ou...  64.2 us
    unnamed x7, local copies, waits for them, and re-layouts  4.41 us

profile of v1, /device:TPU:58, one launch (start us, length us, event | category | flops | bytes accessed | tf_op | source)
XLA Modules:
  0.0 70.6 jit_solution(2387039532687848768)
XLA Ops:
  1.9 0.0 copy-start
  1.9 1.0 %copy-done = bf16[192,1152]{1,0:T(8,128)(2,1)S(1)} copy-done((bf16[192,1152]{1,0:T(8,128)(2,1)S(1)}, bf16[192,1152]{1,0:T(8,128)(2,1)}, u32[]{:S(2)}) %copy-start) | copy-done | bytes 442392
  2.9 0.0 copy-start.1
  2.9 1.0 %copy-done.1 = bf16[192,1152]{1,0:T(8,128)(2,1)S(1)} copy-done((bf16[192,1152]{1,0:T(8,128)(2,1)S(1)}, bf16[192,1152]{1,0:T(8,128)(2,1)}, u32[]{:S(2)}) %copy-start.1) | copy-done | bytes 442392
  4.0 64.2 %band_loss.1 = (f32[192,1152]{1,0:T(8,128)S(1)}, f32[192,1152]{1,0:T(8,128)S(1)}, f32[1,192]{1,0:T(1,128)S(1)}) custom-call(bf16[192,1152]{1,0:T(8,128)(2,1)S(1)} %copy-done, bf16[192,1152]{1,0:T(8,128)(2,1)S(1)} %copy-done.1, f32[1]{0:T(128)S(6)} %copy.10.scale_ref, f32[1]{0:T(128)S(6)} %copy.11.bias_ref), custom_call_target="tpu_custom_call" | custom-call | flops 2038431744 | bytes 2654208 | tf_op jit(solution)/shard_map/band_loss/pallas_call | solution.py:230
  68.2 0.9 %copy.12 = f32[192,1152]{1,0:T(8,128)} copy(f32[192,1152]{1,0:T(8,128)S(1)} %get-tuple-element.12) | data formatting | bytes 1769472
  69.1 0.9 %copy.13 = f32[192,1152]{1,0:T(8,128)} copy(f32[192,1152]{1,0:T(8,128)S(1)} %get-tuple-element.13) | data formatting | bytes 1769472
  70.0 0.6 copy.14
Async XLA Ops:
  1.9 1.0 %copy-start = (bf16[192,1152]{1,0:T(8,128)(2,1)S(1)}, bf16[192,1152]{1,0:T(8,128)(2,1)}, u32[]{:S(2)}) copy-start(bf16[192,1152]{1,0:T(8,128)(2,1)} %img_ref.1) | copy-start | bytes 1327108
  2.9 1.0 %copy-start.1 = (bf16[192,1152]{1,0:T(8,128)(2,1)S(1)}, bf16[192,1152]{1,0:T(8,128)(2,1)}, u32[]{:S(2)}) copy-start(bf16[192,1152]{1,0:T(8,128)(2,1)} %txt_ref.1) | copy-start | bytes 1327108

commit v2 on v1

v2 whole, which is shorter than its diff:
```python
import functools

import jax
import jax.numpy as jnp
from jax import lax
from jax.experimental import pallas as pl
from jax.experimental.pallas import tpu as pltpu
from jax.sharding import PartitionSpec as P

MESH = pl.DeviceIdType.MESH
EPS = 1e-06
PAIRS = 8
PAD = 256
CHUNKS = 2
T1, T2, T3, IM, PA, PB, PX, QS, GS, U1, U2, U3, F2 = range(13)


def kernel(n_blk, n_grp, nc, img_ref, txt_ref, scale_ref, bias_ref, ig_ref, tg_ref, loss_ref,
           xs, tb, sl, gi, pt, ra, rb, rx, rq, s1, s3, sq, sgi, inorm, tnorm, la, ls, lr,
           send_sem, recv_sem, lsend, lrecv):
    blk, grp = lax.axis_index("blk"), lax.axis_index("grp")
    core = lax.rem(grp, 2)
    rows, width = img_ref.shape
    ch = rows // nc
    part = width // 3
    both = jnp.logical_and
    no = jnp.logical_not
    half = n_grp // 2
    chip = lax.rem(grp, half) // 2
    c0, c1 = core == 0, core == 1
    low, high = chip == 0, chip == half // 2 - 1
    low0, low1, high1 = both(low, c0), both(low, c1), both(high, c1)
    one0, six1 = both(chip == 1, c0), both(chip == half // 2 - 2, c1)
    first, last = blk == 0, blk == n_blk - 1

    def to(db, dg):
        return (lax.rem(blk + db + n_blk, n_blk), lax.rem(grp + dg + 2 * n_grp, n_grp))

    def span(c, base=0):
        if isinstance(c, int):
            return pl.ds(base + c * ch, ch)
        return pl.ds(pl.multiple_of(base + c * ch, 16), ch)

    def copy(stream, c, src, dst, target, send=None, at=0):
        return pltpu.make_async_remote_copy(
            src_ref=src.at[span(c)], dst_ref=dst.at[span(c, at)],
            send_sem=send_sem.at[stream if send is None else send, c], recv_sem=recv_sem.at[stream, c],
            device_id=target, device_id_type=MESH)

    def got(stream, c, dst):
        copy(stream, c, dst, dst, to(0, 1)).wait_recv()

    def sent(stream, c, src):
        copy(stream, c, src, src, to(0, 1)).wait_send()

    def each(fn):
        for c in range(nc):
            fn(c)

    barrier = pltpu.get_barrier_semaphore()

    def greet(*targets):
        for db, dg in targets:
            pl.semaphore_signal(barrier, inc=1, device_id=to(db, dg), device_id_type=MESH)

    greet((0, 1), (0, -1), (0, 2), (0, -2))
    pl.when(no(last))(lambda: greet((1, 0)))
    pl.when(no(first))(lambda: greet((-1, 0)))
    pl.when(low0)(lambda: greet((0, -3)))
    pl.when(high1)(lambda: greet((0, 3)))
    pl.when(one0)(lambda: greet((0, -3)))
    pl.when(six1)(lambda: greet((0, 3)))

    def normalize(src, norm, dst):
        def chunk(c, carry):
            r = pl.ds(pl.multiple_of(c * 32, 32), 32)
            v = src[r, :].astype(jnp.float32)
            n = jnp.sqrt(jnp.sum(v * v, axis=1, keepdims=True) + EPS)
            norm[r, :] = n
            dst[r, :] = (v / n).astype(jnp.bfloat16)
            return carry
        lax.fori_loop(0, rows // 32, chunk, 0)

    normalize(txt_ref, tnorm, tb.at[0])
    normalize(img_ref, inorm, xs)
    xs[rows:PAD, :] = jnp.zeros((PAD - rows, width), jnp.bfloat16)
    xs[PAD + rows:, :] = jnp.zeros((PAD - rows, width), jnp.bfloat16)
    extra = jnp.logical_or(jnp.logical_or(low0, high1), jnp.logical_or(one0, six1))
    pl.semaphore_wait(barrier, jnp.where(first, 5, 6) + jnp.where(extra, 1, 0))
    pl.when(first)(lambda: greet((-1, 0)))
    pl.when(last)(lambda: greet((1, 0)))

    @pl.when(high1)
    def _():
        each(lambda c: copy(T3, c, tb.at[0], tb.at[3], to(0, 3), T2).start())

    @pl.when(no(high))
    def _():
        each(lambda c: copy(T2, c, tb.at[0], tb.at[2], to(0, 2)).start())

    def send_images():
        each(lambda c: copy(IM, c, xs, xs, to(-1, 0), at=PAD).start())

    pl.when(no(first))(send_images)

    @pl.when(c0)
    def _():
        each(lambda c: copy(T1, c, tb.at[0], tb.at[1], to(0, 1)).start())

    @pl.when(last)
    def _():
        each(lambda c: copy(GS, c, tb.at[0], tb.at[4], to(1, 0)).start())

    factor = jnp.exp(jnp.full((1, 1), scale_ref[0], jnp.float32))
    bias = bias_ref[0]
    la[...] = jnp.zeros_like(la)

    def score(text, out, lo, hi, diagonal=False):
        logit = lax.dot_general(text, xs[lo:hi, :], (((1,), (1,)), ((), ())), preferred_element_type=jnp.float32)
        x = factor * logit + bias
        minus = 1.0
        if diagonal:
            at = lax.broadcasted_iota(jnp.int32, x.shape, 0)
            to_ = lax.broadcasted_iota(jnp.int32, x.shape, 1)
            minus = jnp.where(at == to_, -1.0, 1.0).astype(jnp.float32)
            x = minus * x
        e = jnp.exp(-jnp.abs(x))
        la[0:1, lo:hi] += jnp.sum(jnp.maximum(x, 0.0) + jnp.log1p(e), axis=0, keepdims=True)
        slope = factor * minus * (jnp.where(x >= 0, 1.0, e) / (1.0 + e))
        out[...] = slope.astype(jnp.bfloat16)

    def text_part(slot, r):
        for n in range(3):
            cols = slice(n * part, (n + 1) * part)
            pt[slot, r, cols] = jnp.dot(sl[slot, r, :], xs[:, cols], preferred_element_type=jnp.float32)

    def image_part(lo, slot, cols):
        return lax.dot_general(
            sl[slot:slot + 4, :, lo:lo + rows].reshape(4 * rows, rows), tb[slot:slot + 4, :, cols].reshape(4 * rows, part),
            (((0,), (0,)), ((), ())), preferred_element_type=jnp.float32)

    def arrive2(c):
        got(T2, c, tb.at[2])

        @pl.when(no(low1))
        def _():
            copy(T3, c, tb.at[2], tb.at[3], to(0, 1)).start()

        @pl.when(c1)
        def _():
            copy(T1, c, tb.at[2], tb.at[1], to(0, -1)).start()

        @pl.when(both(high, c0))
        def _():
            copy(T2, c, tb.at[0], tb.at[2], to(0, 2)).start()

    def arrive3(c):
        got(T3, c, tb.at[3])

        @pl.when(one0)
        def _():
            copy(T2, c, tb.at[3], tb.at[2], to(0, -1), F2).start()

    every = pl.ds(0, rows)
    score(tb[0], sl.at[0, :, 0:PAD], 0, PAD, True)
    pl.when(no(low))(lambda: each(arrive2))
    pl.when(one0)(lambda: each(arrive3))
    each(lambda c: got(IM, c, xs))

    @pl.when(first)
    def _():
        pl.semaphore_wait(barrier, 1)
        send_images()

    def pick(j, values):
        out = jnp.int32(values[-1])
        for i in range(len(values) - 1):
            out = jnp.where(j == i, values[i], out)
        return out

    def combine(c):
        got(PB, c, rb)
        sq[span(c), :] = (pt[2, span(c), :] + rb[span(c), :].astype(jnp.float32)).astype(jnp.bfloat16)
        copy(QS, c, sq, rq, to(0, -2)).start()

    def meet(slot, r, chunks):
        @pl.when(slot == 1)
        def _():
            for c in chunks:
                got(T1, c, tb.at[1])

        @pl.when(both(slot == 3, no(one0)))
        def _():
            for c in chunks:
                arrive3(c)
        score(tb[slot, r, :], sl.at[slot, r, :], 0, 2 * PAD)
        text_part(slot, r)

        @pl.when(slot == 1)
        def _():
            for c in chunks:
                s1[span(c), :] = pt[1, span(c), :].astype(jnp.bfloat16)
                pl.when(c0)(lambda: copy(PB, c, s1, rb, to(0, 1)).start())
                pl.when(c1)(lambda: copy(PA, c, s1, ra, to(0, -1)).start())

        @pl.when(slot == 3)
        def _():
            for c in chunks:
                s3[span(c), :] = pt[3, span(c), :].astype(jnp.bfloat16)
                pl.when(low0)(lambda: copy(PX, c, s3, rx, to(0, -3)).start())
                pl.when(both(c0, no(low)))(lambda: copy(PA, c, s3, ra, to(0, -1)).start())
                pl.when(c1)(lambda: copy(PB, c, s3, rb, to(0, -1)).start())

        @pl.when(both(c0, jnp.where(low, slot == 1, slot == 2)))
        def _():
            for c in chunks:
                combine(c)

    @pl.when(low)
    def _():
        def step(j, carry):
            slot = jnp.where(c0, pick(lax.rem(j, 3), (2, 3, 1)),
                             jnp.where(j < nc, 1, jnp.where(lax.rem(j - nc, 2) == 0, 3, 2)))
            c = jnp.where(c0, j // 3, jnp.where(j < nc, j, (j - nc) // 2))

            @pl.when(jnp.where(c0, slot == 2, slot == 3))
            def _():
                arrive2(c)
            meet(slot, span(c), (c,))
            return carry
        lax.fori_loop(0, 3 * nc, step, 0)

    @pl.when(no(low))
    def _():
        def step(j, carry):
            meet(jnp.where(c0, pick(j, (2, 1, 3)), pick(j, (3, 2, 1))), every, range(nc))
            return carry
        lax.fori_loop(0, 3, step, 0)

    score(tb[0], sl.at[0, :, PAD:], PAD, 2 * PAD)
    ls[...] = la[:, PAD:]
    lcopy = pltpu.make_async_remote_copy(src_ref=ls, dst_ref=lr, send_sem=lsend, recv_sem=lrecv,
                                         device_id=to(1, 0), device_id_type=MESH)

    @pl.when(no(last))
    def _():
        lcopy.start()
        for n in range(3):
            cols = slice(n * part, (n + 1) * part)
            sgi[:, cols] = image_part(PAD, 0, cols).astype(jnp.bfloat16)
        each(lambda c: copy(GS, c, sgi, tb.at[4], to(1, 0)).start())

    text_part(0, every)
    for n in range(3):
        cols = slice(n * part, (n + 1) * part)
        gi[:, cols] = image_part(0, 0, cols)

    @pl.when(first)
    def _():
        for c in range(nc):
            got(GS, c, tb.at[4])
            copy(U2, c, tb.at[4], tb.at[6], to(0, 2)).start()

            @pl.when(c0)
            def _():
                copy(U1, c, tb.at[4], tb.at[5], to(0, 1)).start()

    @pl.when(c1)
    def _():
        for c in range(nc):
            got(PB, c, rb)
            pt[2, span(c), :] += rb[span(c), :].astype(jnp.float32)

            @pl.when(no(high))
            def _():
                got(PA, c, ra)
                pt[2, span(c), :] += ra[span(c), :].astype(jnp.float32)
            sq[span(c), :] = pt[2, span(c), :].astype(jnp.bfloat16)
            copy(QS, c, sq, rq, to(0, -2)).start()

    @pl.when(first)
    def _():
        for c in range(nc):
            got(U2, c, tb.at[6])
            copy(U3, c, tb.at[6], tb.at[7], to(0, 1)).start()

            @pl.when(c1)
            def _():
                copy(U1, c, tb.at[6], tb.at[5], to(0, -1)).start()

        def seam(j, carry):
            slot = jnp.where(c0, pick(j, (4, 6, 5, 7)), pick(j, (4, 5, 6, 7)))

            @pl.when(slot == 5)
            def _():
                each(lambda c: got(U1, c, tb.at[5]))

            @pl.when(slot == 7)
            def _():
                each(lambda c: got(U3, c, tb.at[7]))
            score(tb[slot], sl.at[slot, :, 0:PAD], 0, PAD)
            return carry
        lax.fori_loop(0, 4, seam, 0)
        for n in range(3):
            cols = slice(n * part, (n + 1) * part)
            gi[:, cols] += image_part(0, 4, cols)
        for c in range(nc):
            sent(U1, c, tb.at[4])
            sent(U2, c, tb.at[4])
            sent(U3, c, tb.at[6])

    @pl.when(c0)
    def _():
        for c in range(nc):
            got(PA, c, ra)
            pt[0, span(c), :] += ra[span(c), :].astype(jnp.float32)

    @pl.when(six1)
    def _():
        for c in range(nc):
            got(PX, c, rx)
            pt[0, span(c), :] += rx[span(c), :].astype(jnp.float32)

    def back(c, src, norm, hat, out):
        n = norm[span(c), :]
        unit = src[span(c), :].astype(jnp.float32) / n
        along = jnp.sum(unit * hat, axis=1, keepdims=True)
        out[span(c), :] = (hat - unit * along) / n

    for c in range(nc):
        @pl.when(no(first))
        def _():
            got(GS, c, tb.at[4])
            gi[span(c), :] += tb[4, span(c), :].astype(jnp.float32)
        back(c, img_ref, inorm, gi[span(c), :], ig_ref)

    @pl.when(no(first))
    def _():
        lcopy.wait_recv()
        la[:, 0:PAD] += lr[...]
    loss_ref[...] = la[0:1, 0:rows] / (PAIRS * rows)
    for c in range(nc):
        got(QS, c, rq)
        back(c, txt_ref, tnorm, pt[0, span(c), :] + rq[span(c), :].astype(jnp.float32), tg_ref)

    for c in range(nc):
        sent(T1, c, tb.at[1])
        sent(IM, c, xs)
        sent(PB, c, s3)
        sent(GS, c, sgi)
        sent(T2, c, tb.at[0])
        sent(QS, c, sq)
        pl.when(one0)(lambda: sent(F2, c, tb.at[3]))
        pl.when(no(low1))(lambda: sent(T3, c, tb.at[2]))

        pl.when(low0)(lambda: sent(PX, c, s3))
        pl.when(no(low0))(lambda: sent(PA, c, s3))

    @pl.when(no(last))
    def _():
        lcopy.wait_send()


def solution(mesh):
    n_blk, n_grp = mesh.shape["blk"], mesh.shape["grp"]

    def body(image_embed, text_embed, log_scale, logit_bias):
        rows, width = image_embed.shape
        nc = CHUNKS
        half = lambda *shape: pltpu.VMEM(shape, jnp.bfloat16)
        full = lambda *shape: pltpu.VMEM(shape, jnp.float32)
        dma = pltpu.SemaphoreType.DMA
        vmem = pl.BlockSpec(memory_space=pltpu.VMEM)
        smem = pl.BlockSpec(memory_space=pltpu.SMEM)
        out = lambda *shape: jax.ShapeDtypeStruct(shape, jnp.float32)
        image_grad, text_grad, loss = pl.pallas_call(
            functools.partial(kernel, n_blk, n_grp, nc),
            out_shape=(out(rows, width), out(rows, width), out(1, rows)),
            in_specs=[vmem, vmem, smem, smem],
            out_specs=(vmem, vmem, vmem),
            scratch_shapes=[
                half(2 * PAD, width), half(8, rows, width), half(8, rows, 2 * PAD), full(rows, width),
                full(4, rows, width), *[half(rows, width)] * 8,
                full(rows, 1), full(rows, 1), full(8, 2 * PAD), full(8, PAD), full(8, PAD),
                dma((13, nc)), dma((12, nc)), dma, dma,
            ],
            compiler_params=pltpu.CompilerParams(
                collective_id=0, has_side_effects=True, vmem_limit_bytes=40 << 20),
            cost_estimate=pl.CostEstimate(flops=48 * rows * rows * width, bytes_accessed=12 * rows * width,
                                          transcendentals=24 * rows * rows),
            name="band_loss",
        )(image_embed, text_embed, log_scale, logit_bias)
        return image_grad, text_grad, loss.reshape(rows)

    in_specs = (P(("blk", "grp"), None), P(("blk", "grp"), None), P(), P())
    out_specs = (P(("blk", "grp"), None), P(("blk", "grp"), None), P(("blk", "grp")))
    return jax.shard_map(body, mesh=mesh, in_specs=in_specs, out_specs=out_specs, check_vma=False)
```

time: 70.8 us -> 71.8 us (1.014)
  the two profiles are of different devices: /device:TPU:58 before, /device:TPU:1 now
where the time goes in v2:
time: 71.8 us; the launch traced here: 70.5 us
  Pallas kernels  64.2 us (89%)
  local copies, waits for them, and re-layouts  4.41 us (6%)
  between operations  1.94 us (3%)
    pallas_call x1, Pallas kernels, body(): pl.pallas_call(functools.partial(kernel, n_blk, n_grp, nc), out_shape=(ou...  64.2 us
    unnamed x7, local copies, waits for them, and re-layouts  4.41 us

profile of v2, /device:TPU:1, one launch (start us, length us, event | category | flops | bytes accessed | tf_op | source)
XLA Modules:
  0.0 70.5 jit_solution(15951567842156795434)
XLA Ops:
  1.9 0.0 copy-start
  1.9 1.0 %copy-done = bf16[192,1152]{1,0:T(8,128)(2,1)S(1)} copy-done((bf16[192,1152]{1,0:T(8,128)(2,1)S(1)}, bf16[192,1152]{1,0:T(8,128)(2,1)}, u32[]{:S(2)}) %copy-start) | copy-done | bytes 442392
  2.9 0.0 copy-start.1
  2.9 1.0 %copy-done.1 = bf16[192,1152]{1,0:T(8,128)(2,1)S(1)} copy-done((bf16[192,1152]{1,0:T(8,128)(2,1)S(1)}, bf16[192,1152]{1,0:T(8,128)(2,1)}, u32[]{:S(2)}) %copy-start.1) | copy-done | bytes 442392
  4.0 64.2 %band_loss.1 = (f32[192,1152]{1,0:T(8,128)S(1)}, f32[192,1152]{1,0:T(8,128)S(1)}, f32[1,192]{1,0:T(1,128)S(1)}) custom-call(bf16[192,1152]{1,0:T(8,128)(2,1)S(1)} %copy-done, bf16[192,1152]{1,0:T(8,128)(2,1)S(1)} %copy-done.1, f32[1]{0:T(128)S(6)} %copy.10.scale_ref, f32[1]{0:T(128)S(6)} %copy.11.bias_ref), custom_call_target="tpu_custom_call" | custom-call | flops 2038431744 | bytes 2654208 | tf_op jit(solution)/shard_map/band_loss/pallas_call | solution.py:376
  68.1 0.9 %copy.12 = f32[192,1152]{1,0:T(8,128)} copy(f32[192,1152]{1,0:T(8,128)S(1)} %get-tuple-element.12) | data formatting | bytes 1769472
  69.0 0.9 %copy.13 = f32[192,1152]{1,0:T(8,128)} copy(f32[192,1152]{1,0:T(8,128)S(1)} %get-tuple-element.13) | data formatting | bytes 1769472
  69.9 0.6 copy.14
Async XLA Ops:
  1.9 1.0 %copy-start = (bf16[192,1152]{1,0:T(8,128)(2,1)S(1)}, bf16[192,1152]{1,0:T(8,128)(2,1)}, u32[]{:S(2)}) copy-start(bf16[192,1152]{1,0:T(8,128)(2,1)} %img_ref.1) | copy-start | bytes 1327108
  2.9 1.0 %copy-start.1 = (bf16[192,1152]{1,0:T(8,128)(2,1)S(1)}, bf16[192,1152]{1,0:T(8,128)(2,1)}, u32[]{:S(2)}) copy-start(bf16[192,1152]{1,0:T(8,128)(2,1)} %txt_ref.1) | copy-start | bytes 1327108

commit v3 on v2

--- a/solution.py
+++ b/solution.py
@@ -12,11 +12,11 @@
 PAIRS = 8
 PAD = 256
 CHUNKS = 2
-T1, T2, T3, IM, PA, PB, PX, QS, GS, U1, U2, U3, F2 = range(13)
+T1, T2, T3, IM, PA, PB, PX, QS, GS, U1, U2, U3, W2, F2, F4 = range(15)
 
 
 def kernel(n_blk, n_grp, nc, img_ref, txt_ref, scale_ref, bias_ref, ig_ref, tg_ref, loss_ref,
-           xs, tb, sl, gi, pt, ra, rb, rx, rq, s1, s3, sq, sgi, inorm, tnorm, la, ls, lr,
+           xs, tb, sl, gi, pt, ra, rb, rx, rq, s1, s3, sq, sgi, w2, inorm, tnorm, la, ls, lr,
            send_sem, recv_sem, lsend, lrecv):
     blk, grp = lax.axis_index("blk"), lax.axis_index("grp")
     core = lax.rem(grp, 2)
@@ -29,7 +29,7 @@
     chip = lax.rem(grp, half) // 2
     c0, c1 = core == 0, core == 1
     low, high = chip == 0, chip == half // 2 - 1
-    low0, low1, high1 = both(low, c0), both(low, c1), both(high, c1)
+    low0, low1, high0, high1 = both(low, c0), both(low, c1), both(high, c0), both(high, c1)
     one0, six1 = both(chip == 1, c0), both(chip == half // 2 - 2, c1)
     first, last = blk == 0, blk == n_blk - 1
 
@@ -66,7 +66,8 @@
     greet((0, 1), (0, -1), (0, 2), (0, -2))
     pl.when(no(last))(lambda: greet((1, 0)))
     pl.when(no(first))(lambda: greet((-1, 0)))
-    pl.when(low0)(lambda: greet((0, -3)))
+    pl.when(low0)(lambda: greet((0, -3), (0, -2 - half)))
+    pl.when(high0)(lambda: greet((0, half), (0, 2 + half)))
     pl.when(high1)(lambda: greet((0, 3)))
     pl.when(one0)(lambda: greet((0, -3)))
     pl.when(six1)(lambda: greet((0, 3)))
@@ -85,11 +86,15 @@
     normalize(img_ref, inorm, xs)
     xs[rows:PAD, :] = jnp.zeros((PAD - rows, width), jnp.bfloat16)
     xs[PAD + rows:, :] = jnp.zeros((PAD - rows, width), jnp.bfloat16)
-    extra = jnp.logical_or(jnp.logical_or(low0, high1), jnp.logical_or(one0, six1))
-    pl.semaphore_wait(barrier, jnp.where(first, 5, 6) + jnp.where(extra, 1, 0))
+    extra = jnp.where(jnp.logical_or(low0, high0), 2, jnp.where(jnp.logical_or(high1, jnp.logical_or(one0, six1)), 1, 0))
+    pl.semaphore_wait(barrier, jnp.where(first, 5, 6) + extra)
     pl.when(first)(lambda: greet((-1, 0)))
     pl.when(last)(lambda: greet((1, 0)))
 
+    @pl.when(high0)
+    def _():
+        each(lambda c: copy(W2, c, tb.at[0], w2, to(0, half)).start())
+
     @pl.when(high1)
     def _():
         each(lambda c: copy(T3, c, tb.at[0], tb.at[3], to(0, 3), T2).start())
@@ -100,6 +105,10 @@
 
     def send_images():
         each(lambda c: copy(IM, c, xs, xs, to(-1, 0), at=PAD).start())
+
+    def late_images():
+        pl.semaphore_wait(barrier, 1)
+        send_images()
 
     pl.when(no(first))(send_images)
 
@@ -150,9 +159,10 @@
         def _():
             copy(T1, c, tb.at[2], tb.at[1], to(0, -1)).start()
 
-        @pl.when(both(high, c0))
-        def _():
-            copy(T2, c, tb.at[0], tb.at[2], to(0, 2)).start()
+        @pl.when(high0)
+        def _():
+            got(W2, c, w2)
+            copy(T2, c, w2, tb.at[2], to(0, 2 + half), F2).start()
 
     def arrive3(c):
         got(T3, c, tb.at[3])
@@ -160,17 +170,31 @@
         @pl.when(one0)
         def _():
             copy(T2, c, tb.at[3], tb.at[2], to(0, -1), F2).start()
+
+    def seam_start():
+        for c in range(nc):
+            got(GS, c, tb.at[4])
+
+            @pl.when(high1)
+            def _():
+                copy(U3, c, tb.at[4], tb.at[7], to(0, 3), U2).start()
+
+            @pl.when(no(high1))
+            def _():
+                copy(U2, c, tb.at[4], tb.at[6], to(0, 2)).start()
+
+            @pl.when(c0)
+            def _():
+                copy(U1, c, tb.at[4], tb.at[5], to(0, 1)).start()
 
     every = pl.ds(0, rows)
     score(tb[0], sl.at[0, :, 0:PAD], 0, PAD, True)
     pl.when(no(low))(lambda: each(arrive2))
     pl.when(one0)(lambda: each(arrive3))
+    pl.when(both(first, low))(late_images)
     each(lambda c: got(IM, c, xs))
 
-    @pl.when(first)
-    def _():
-        pl.semaphore_wait(barrier, 1)
-        send_images()
+    pl.when(both(first, no(low)))(late_images)
 
     def pick(j, values):
         out = jnp.int32(values[-1])
@@ -237,6 +261,7 @@
             return carry
         lax.fori_loop(0, 3, step, 0)
 
+    pl.when(both(first, low))(seam_start)
     score(tb[0], sl.at[0, :, PAD:], PAD, 2 * PAD)
     ls[...] = la[:, PAD:]
     lcopy = pltpu.make_async_remote_copy(src_ref=ls, dst_ref=lr, send_sem=lsend, recv_sem=lrecv,
@@ -255,15 +280,7 @@
         cols = slice(n * part, (n + 1) * part)
         gi[:, cols] = image_part(0, 0, cols)
 
-    @pl.when(first)
-    def _():
-        for c in range(nc):
-            got(GS, c, tb.at[4])
-            copy(U2, c, tb.at[4], tb.at[6], to(0, 2)).start()
-
-            @pl.when(c0)
-            def _():
-                copy(U1, c, tb.at[4], tb.at[5], to(0, 1)).start()
+    pl.when(both(first, no(low)))(seam_start)
 
     @pl.when(c1)
     def _():
@@ -281,8 +298,15 @@
     @pl.when(first)
     def _():
         for c in range(nc):
+            @pl.when(one0)
+            def _():
+                got(U3, c, tb.at[7])
+                copy(U2, c, tb.at[7], tb.at[6], to(0, -1), F4).start()
             got(U2, c, tb.at[6])
-            copy(U3, c, tb.at[6], tb.at[7], to(0, 1)).start()
+
+            @pl.when(no(low1))
+            def _():
+                copy(U3, c, tb.at[6], tb.at[7], to(0, 1)).start()
 
             @pl.when(c1)
             def _():
@@ -295,7 +319,7 @@
             def _():
                 each(lambda c: got(U1, c, tb.at[5]))
 
-            @pl.when(slot == 7)
+            @pl.when(both(slot == 7, no(one0)))
             def _():
                 each(lambda c: got(U3, c, tb.at[7]))
             score(tb[slot], sl.at[slot, :, 0:PAD], 0, PAD)
@@ -307,7 +331,8 @@
         for c in range(nc):
             sent(U1, c, tb.at[4])
             sent(U2, c, tb.at[4])
-            sent(U3, c, tb.at[6])
+            pl.when(no(low1))(lambda: sent(U3, c, tb.at[6]))
+            pl.when(one0)(lambda: sent(F4, c, tb.at[7]))
 
     @pl.when(c0)
     def _():
@@ -348,9 +373,10 @@
         sent(IM, c, xs)
         sent(PB, c, s3)
         sent(GS, c, sgi)
-        sent(T2, c, tb.at[0])
+        pl.when(high0)(lambda: sent(W2, c, tb.at[0]))
+        pl.when(no(high0))(lambda: sent(T2, c, tb.at[0]))
         sent(QS, c, sq)
-        pl.when(one0)(lambda: sent(F2, c, tb.at[3]))
+        pl.when(jnp.logical_or(one0, high0))(lambda: sent(F2, c, tb.at[3]))
         pl.when(no(low1))(lambda: sent(T3, c, tb.at[2]))
 
         pl.when(low0)(lambda: sent(PX, c, s3))
@@ -380,9 +406,9 @@
             out_specs=(vmem, vmem, vmem),
             scratch_shapes=[
                 half(2 * PAD, width), half(8, rows, width), half(8, rows, 2 * PAD), full(rows, width),
-                full(4, rows, width), *[half(rows, width)] * 8,
+                full(4, rows, width), *[half(rows, width)] * 9,
                 full(rows, 1), full(rows, 1), full(8, 2 * PAD), full(8, PAD), full(8, PAD),
-                dma((13, nc)), dma((12, nc)), dma, dma,
+                dma((15, nc)), dma((13, nc)), dma, dma,
             ],
             compiler_params=pltpu.CompilerParams(
                 collective_id=0, has_side_effects=True, vmem_limit_bytes=40 << 20),

time: 71.8 us -> 64.3 us (0.90); the launches traced: 70.5 us -> 64 us
  Pallas kernels: 64.2 us -> 57.7 us
    pallas_call x1, Pallas kernels: 64.2 us -> 57.7 us  [body(): pl.pallas_call(functools.partial(kernel, n_blk, n_grp, nc), out_shape=(ou...]
where the time goes in v3:
time: 64.3 us; the launch traced here: 64 us
  Pallas kernels  57.7 us (90%)
  local copies, waits for them, and re-layouts  4.41 us (7%)
  between operations  1.94 us (3%)
    pallas_call x1, Pallas kernels, body(): pl.pallas_call(functools.partial(kernel, n_blk, n_grp, nc), out_shape=(ou...  57.7 us
    unnamed x7, local copies, waits for them, and re-layouts  4.41 us

profile of v3, /device:TPU:1, one launch (start us, length us, event | category | flops | bytes accessed | tf_op | source)
XLA Modules:
  0.0 64.0 jit_solution(17395819727276392926)
XLA Ops:
  1.9 0.0 copy-start
  1.9 1.0 %copy-done = bf16[192,1152]{1,0:T(8,128)(2,1)S(1)} copy-done((bf16[192,1152]{1,0:T(8,128)(2,1)S(1)}, bf16[192,1152]{1,0:T(8,128)(2,1)}, u32[]{:S(2)}) %copy-start) | copy-done | bytes 442392
  2.9 0.0 copy-start.1
  2.9 1.0 %copy-done.1 = bf16[192,1152]{1,0:T(8,128)(2,1)S(1)} copy-done((bf16[192,1152]{1,0:T(8,128)(2,1)S(1)}, bf16[192,1152]{1,0:T(8,128)(2,1)}, u32[]{:S(2)}) %copy-start.1) | copy-done | bytes 442392
  4.0 57.7 %band_loss.1 = (f32[192,1152]{1,0:T(8,128)S(1)}, f32[192,1152]{1,0:T(8,128)S(1)}, f32[1,192]{1,0:T(1,128)S(1)}) custom-call(bf16[192,1152]{1,0:T(8,128)(2,1)S(1)} %copy-done, bf16[192,1152]{1,0:T(8,128)(2,1)S(1)} %copy-done.1, f32[1]{0:T(128)S(6)} %copy.10.scale_ref, f32[1]{0:T(128)S(6)} %copy.11.bias_ref), custom_call_target="tpu_custom_call" | custom-call | flops 2038431744 | bytes 2654208 | tf_op jit(solution)/shard_map/band_loss/pallas_call | solution.py:402
  61.6 0.9 %copy.12 = f32[192,1152]{1,0:T(8,128)} copy(f32[192,1152]{1,0:T(8,128)S(1)} %get-tuple-element.12) | data formatting | bytes 1769472
  62.5 0.9 %copy.13 = f32[192,1152]{1,0:T(8,128)} copy(f32[192,1152]{1,0:T(8,128)S(1)} %get-tuple-element.13) | data formatting | bytes 1769472
  63.5 0.6 copy.14
Async XLA Ops:
  1.9 1.0 %copy-start = (bf16[192,1152]{1,0:T(8,128)(2,1)S(1)}, bf16[192,1152]{1,0:T(8,128)(2,1)}, u32[]{:S(2)}) copy-start(bf16[192,1152]{1,0:T(8,128)(2,1)} %img_ref.1) | copy-start | bytes 1327108
  2.9 1.0 %copy-start.1 = (bf16[192,1152]{1,0:T(8,128)(2,1)S(1)}, bf16[192,1152]{1,0:T(8,128)(2,1)}, u32[]{:S(2)}) copy-start(bf16[192,1152]{1,0:T(8,128)(2,1)} %txt_ref.1) | copy-start | bytes 1327108

commit v4 on v3

--- a/solution.py
+++ b/solution.py
@@ -32,6 +32,10 @@
     low0, low1, high0, high1 = both(low, c0), both(low, c1), both(high, c0), both(high, c1)
     one0, six1 = both(chip == 1, c0), both(chip == half // 2 - 2, c1)
     first, last = blk == 0, blk == n_blk - 1
+    origin = both(first, grp == 0)
+    near = functools.reduce(jnp.logical_or, [grp == k for k in (1, 2, half - 2, n_grp - 2, n_grp - 1)])
+    near = both(first, near)
+    near_blk, near_six = both(blk == 1, grp == 0), both(first, grp == n_grp - 3)
 
     def to(db, dg):
         return (lax.rem(blk + db + n_blk, n_blk), lax.rem(grp + dg + 2 * n_grp, n_grp))
@@ -63,14 +67,19 @@
         for db, dg in targets:
             pl.semaphore_signal(barrier, inc=1, device_id=to(db, dg), device_id_type=MESH)
 
-    greet((0, 1), (0, -1), (0, 2), (0, -2))
-    pl.when(no(last))(lambda: greet((1, 0)))
-    pl.when(no(first))(lambda: greet((-1, 0)))
-    pl.when(low0)(lambda: greet((0, -3), (0, -2 - half)))
-    pl.when(high0)(lambda: greet((0, half), (0, 2 + half)))
+    early = no(origin)
+    for step_ in (1, -1, 2, -2):
+        pl.when(both(early, no(both(first, lax.rem(grp + step_ + n_grp, n_grp) == 0))))(
+            functools.partial(greet, (0, step_)))
+    pl.when(both(early, no(last)))(lambda: greet((1, 0)))
+    pl.when(no(jnp.logical_or(first, near_blk)))(lambda: greet((-1, 0)))
+    pl.when(both(early, low0))(lambda: greet((0, -3), (0, -2 - half)))
+    pl.when(high0)(lambda: greet((0, half)))
+    pl.when(both(high0, no(near)))(lambda: greet((0, 2 + half)))
+    pl.when(both(high0, both(near, grp != half - 2)))(lambda: greet((0, 2 + half)))
     pl.when(high1)(lambda: greet((0, 3)))
     pl.when(one0)(lambda: greet((0, -3)))
-    pl.when(six1)(lambda: greet((0, 3)))
+    pl.when(both(six1, no(near_six)))(lambda: greet((0, 3)))
 
     def normalize(src, norm, dst):
         def chunk(c, carry):
@@ -87,9 +96,13 @@
     xs[rows:PAD, :] = jnp.zeros((PAD - rows, width), jnp.bfloat16)
     xs[PAD + rows:, :] = jnp.zeros((PAD - rows, width), jnp.bfloat16)
     extra = jnp.where(jnp.logical_or(low0, high0), 2, jnp.where(jnp.logical_or(high1, jnp.logical_or(one0, six1)), 1, 0))
-    pl.semaphore_wait(barrier, jnp.where(first, 5, 6) + extra)
+    fewer = jnp.where(jnp.logical_or(near, jnp.logical_or(near_blk, near_six)), 1, 0)
+    pl.semaphore_wait(barrier, jnp.where(first, 5, 6) + extra - fewer)
     pl.when(first)(lambda: greet((-1, 0)))
     pl.when(last)(lambda: greet((1, 0)))
+    pl.when(jnp.logical_or(near, near_six))(lambda: greet((0, n_grp - grp)))
+    pl.when(near_blk)(lambda: greet((-1, 0)))
+    pl.when(origin)(lambda: greet((0, 1), (0, -1), (0, 2), (0, -2), (0, half - 2), (1, 0)))
 
     @pl.when(high0)
     def _():
@@ -107,18 +120,20 @@
         each(lambda c: copy(IM, c, xs, xs, to(-1, 0), at=PAD).start())
 
     def late_images():
-        pl.semaphore_wait(barrier, 1)
+        pl.semaphore_wait(barrier, jnp.where(near, 2, 1))
         send_images()
 
-    pl.when(no(first))(send_images)
+    pl.when(no(jnp.logical_or(first, near_blk)))(send_images)
 
     @pl.when(c0)
     def _():
         each(lambda c: copy(T1, c, tb.at[0], tb.at[1], to(0, 1)).start())
 
-    @pl.when(last)
-    def _():
-        each(lambda c: copy(GS, c, tb.at[0], tb.at[4], to(1, 0)).start())
+    def send_seam(c):
+        copy(GS, c, tb.at[0], tb.at[4], to(1, 0)).start()
+
+    pl.when(both(last, low))(lambda: send_seam(0))
+    pl.when(both(last, no(low)))(lambda: each(send_seam))
 
     factor = jnp.exp(jnp.full((1, 1), scale_ref[0], jnp.float32))
     bias = bias_ref[0]
@@ -151,18 +166,13 @@
     def arrive2(c):
         got(T2, c, tb.at[2])
 
-        @pl.when(no(low1))
+        @pl.when(no(jnp.logical_or(low1, both(near, high1))))
         def _():
             copy(T3, c, tb.at[2], tb.at[3], to(0, 1)).start()
 
         @pl.when(c1)
         def _():
             copy(T1, c, tb.at[2], tb.at[1], to(0, -1)).start()
-
-        @pl.when(high0)
-        def _():
-            got(W2, c, w2)
-            copy(T2, c, w2, tb.at[2], to(0, 2 + half), F2).start()
 
     def arrive3(c):
         got(T3, c, tb.at[3])
@@ -171,30 +181,52 @@
         def _():
             copy(T2, c, tb.at[3], tb.at[2], to(0, -1), F2).start()
 
+    def seam_chunk(c):
+        got(GS, c, tb.at[4])
+
+        @pl.when(high1)
+        def _():
+            copy(U3, c, tb.at[4], tb.at[7], to(0, 3), U2).start()
+
+        @pl.when(no(high1))
+        def _():
+            copy(U2, c, tb.at[4], tb.at[6], to(0, 2)).start()
+
+        @pl.when(c0)
+        def _():
+            copy(U1, c, tb.at[4], tb.at[5], to(0, 1)).start()
+
     def seam_start():
-        for c in range(nc):
-            got(GS, c, tb.at[4])
-
-            @pl.when(high1)
-            def _():
-                copy(U3, c, tb.at[4], tb.at[7], to(0, 3), U2).start()
-
-            @pl.when(no(high1))
-            def _():
-                copy(U2, c, tb.at[4], tb.at[6], to(0, 2)).start()
-
-            @pl.when(c0)
-            def _():
-                copy(U1, c, tb.at[4], tb.at[5], to(0, 1)).start()
+        each(seam_chunk)
 
     every = pl.ds(0, rows)
     score(tb[0], sl.at[0, :, 0:PAD], 0, PAD, True)
     pl.when(no(low))(lambda: each(arrive2))
+
+    def relay():
+        for c in range(nc):
+            got(W2, c, w2)
+            copy(T2, c, w2, tb.at[2], to(0, 2 + half), F2).start()
+
+    before_origin = both(first, grp == half - 2)
+    pl.when(both(high0, no(before_origin)))(relay)
     pl.when(one0)(lambda: each(arrive3))
-    pl.when(both(first, low))(late_images)
-    each(lambda c: got(IM, c, xs))
+    pl.when(jnp.logical_or(both(near, low), near_blk))(late_images)
+    got(IM, 0, xs)
+
+    @pl.when(both(last, low))
+    def _():
+        for c in range(1, nc):
+            send_seam(c)
+    for c in range(1, nc):
+        got(IM, c, xs)
 
     pl.when(both(first, no(low)))(late_images)
+    pl.when(before_origin)(relay)
+
+    @pl.when(both(high1, near))
+    def _():
+        each(lambda c: copy(T3, c, tb.at[2], tb.at[3], to(0, 1)).start())
 
     def pick(j, values):
         out = jnp.int32(values[-1])
@@ -251,6 +283,10 @@
             def _():
                 arrive2(c)
             meet(slot, span(c), (c,))
+            pl.when(both(both(first, no(near)), j == 1))(late_images)
+
+            for k in range(nc):
+                pl.when(both(first, j == 2 + 3 * k))(functools.partial(seam_chunk, k))
             return carry
         lax.fori_loop(0, 3 * nc, step, 0)
 
@@ -261,7 +297,6 @@
             return carry
         lax.fori_loop(0, 3, step, 0)
 
-    pl.when(both(first, low))(seam_start)
     score(tb[0], sl.at[0, :, PAD:], PAD, 2 * PAD)
     ls[...] = la[:, PAD:]
     lcopy = pltpu.make_async_remote_copy(src_ref=ls, dst_ref=lr, send_sem=lsend, recv_sem=lrecv,
@@ -295,13 +330,15 @@
             sq[span(c), :] = pt[2, span(c), :].astype(jnp.bfloat16)
             copy(QS, c, sq, rq, to(0, -2)).start()
 
+    @pl.when(both(first, one0))
+    def _():
+        for c in range(nc):
+            got(U3, c, tb.at[7])
+            copy(U2, c, tb.at[7], tb.at[6], to(0, -1), F4).start()
+
     @pl.when(first)
     def _():
         for c in range(nc):
-            @pl.when(one0)
-            def _():
-                got(U3, c, tb.at[7])
-                copy(U2, c, tb.at[7], tb.at[6], to(0, -1), F4).start()
             got(U2, c, tb.at[6])
 
             @pl.when(no(low1))

time: 64.3 us -> 62.3 us (0.969)
  the two profiles are of different devices: /device:TPU:1 before, /device:TPU:2 now
where the time goes in v4:
time: 62.3 us; the launch traced here: 62.1 us
  Pallas kernels  55.7 us (89%)
  local copies, waits for them, and re-layouts  4.41 us (7%)
  between operations  1.94 us (3%)
    pallas_call x1, Pallas kernels, body(): pl.pallas_call(functools.partial(kernel, n_blk, n_grp, nc), out_shape=(ou...  55.7 us
    unnamed x7, local copies, waits for them, and re-layouts  4.41 us

profile of v4, /device:TPU:2, one launch (start us, length us, event | category | flops | bytes accessed | tf_op | source)
XLA Modules:
  0.0 62.1 jit_solution(9031030976095316169)
XLA Ops:
  1.9 0.0 copy-start
  1.9 1.0 %copy-done = bf16[192,1152]{1,0:T(8,128)(2,1)S(1)} copy-done((bf16[192,1152]{1,0:T(8,128)(2,1)S(1)}, bf16[192,1152]{1,0:T(8,128)(2,1)}, u32[]{:S(2)}) %copy-start) | copy-done | bytes 442392
  2.9 0.0 copy-start.1
  2.9 1.0 %copy-done.1 = bf16[192,1152]{1,0:T(8,128)(2,1)S(1)} copy-done((bf16[192,1152]{1,0:T(8,128)(2,1)S(1)}, bf16[192,1152]{1,0:T(8,128)(2,1)}, u32[]{:S(2)}) %copy-start.1) | copy-done | bytes 442392
  4.0 55.7 %band_loss.1 = (f32[192,1152]{1,0:T(8,128)S(1)}, f32[192,1152]{1,0:T(8,128)S(1)}, f32[1,192]{1,0:T(1,128)S(1)}) custom-call(bf16[192,1152]{1,0:T(8,128)(2,1)S(1)} %copy-done, bf16[192,1152]{1,0:T(8,128)(2,1)S(1)} %copy-done.1, f32[1]{0:T(128)S(6)} %copy.10.scale_ref, f32[1]{0:T(128)S(6)} %copy.11.bias_ref), custom_call_target="tpu_custom_call" | custom-call | flops 2038431744 | bytes 2654208 | tf_op jit(solution)/shard_map/band_loss/pallas_call | solution.py:439
  59.7 0.9 %copy.12 = f32[192,1152]{1,0:T(8,128)} copy(f32[192,1152]{1,0:T(8,128)S(1)} %get-tuple-element.12) | data formatting | bytes 1769472
  60.6 0.9 %copy.13 = f32[192,1152]{1,0:T(8,128)} copy(f32[192,1152]{1,0:T(8,128)S(1)} %get-tuple-element.13) | data formatting | bytes 1769472
  61.5 0.6 copy.14
Async XLA Ops:
  1.9 1.0 %copy-start = (bf16[192,1152]{1,0:T(8,128)(2,1)S(1)}, bf16[192,1152]{1,0:T(8,128)(2,1)}, u32[]{:S(2)}) copy-start(bf16[192,1152]{1,0:T(8,128)(2,1)} %img_ref.1) | copy-start | bytes 1327108
  2.9 1.0 %copy-start.1 = (bf16[192,1152]{1,0:T(8,128)(2,1)S(1)}, bf16[192,1152]{1,0:T(8,128)(2,1)}, u32[]{:S(2)}) copy-start(bf16[192,1152]{1,0:T(8,128)(2,1)} %txt_ref.1) | copy-start | bytes 1327108

commit v5 on v4

--- a/solution.py
+++ b/solution.py
@@ -91,18 +91,22 @@
             return carry
         lax.fori_loop(0, rows // 32, chunk, 0)
 
+    def enter():
+        extra = jnp.where(jnp.logical_or(low0, high0), 2, jnp.where(jnp.logical_or(high1, jnp.logical_or(one0, six1)), 1, 0))
+        fewer = jnp.where(jnp.logical_or(near, jnp.logical_or(near_blk, near_six)), 1, 0)
+        pl.semaphore_wait(barrier, jnp.where(first, 5, 6) + extra - fewer)
+        pl.when(first)(lambda: greet((-1, 0)))
+        pl.when(last)(lambda: greet((1, 0)))
+        pl.when(jnp.logical_or(near, near_six))(lambda: greet((0, n_grp - grp)))
+        pl.when(near_blk)(lambda: greet((-1, 0)))
+        pl.when(origin)(lambda: greet((0, 1), (0, -1), (0, 2), (0, -2), (0, half - 2), (1, 0)))
+
+    pl.when(origin)(enter)
     normalize(txt_ref, tnorm, tb.at[0])
     normalize(img_ref, inorm, xs)
     xs[rows:PAD, :] = jnp.zeros((PAD - rows, width), jnp.bfloat16)
     xs[PAD + rows:, :] = jnp.zeros((PAD - rows, width), jnp.bfloat16)
-    extra = jnp.where(jnp.logical_or(low0, high0), 2, jnp.where(jnp.logical_or(high1, jnp.logical_or(one0, six1)), 1, 0))
-    fewer = jnp.where(jnp.logical_or(near, jnp.logical_or(near_blk, near_six)), 1, 0)
-    pl.semaphore_wait(barrier, jnp.where(first, 5, 6) + extra - fewer)
-    pl.when(first)(lambda: greet((-1, 0)))
-    pl.when(last)(lambda: greet((1, 0)))
-    pl.when(jnp.logical_or(near, near_six))(lambda: greet((0, n_grp - grp)))
-    pl.when(near_blk)(lambda: greet((-1, 0)))
-    pl.when(origin)(lambda: greet((0, 1), (0, -1), (0, 2), (0, -2), (0, half - 2), (1, 0)))
+    pl.when(no(origin))(enter)
 
     @pl.when(high0)
     def _():
@@ -272,6 +276,11 @@
             for c in chunks:
                 combine(c)
 
+    def score_own():
+        score(tb[0], sl.at[0, :, PAD:], PAD, 2 * PAD)
+
+    pl.when(low)(score_own)
+
     @pl.when(low)
     def _():
         def step(j, carry):
@@ -297,7 +306,7 @@
             return carry
         lax.fori_loop(0, 3, step, 0)
 
-    score(tb[0], sl.at[0, :, PAD:], PAD, 2 * PAD)
+    pl.when(no(low))(score_own)
     ls[...] = la[:, PAD:]
     lcopy = pltpu.make_async_remote_copy(src_ref=ls, dst_ref=lr, send_sem=lsend, recv_sem=lrecv,
                                          device_id=to(1, 0), device_id_type=MESH)

time: 62.3 us -> 62 us (level)
  the two profiles are of different devices: /device:TPU:2 before, /device:TPU:1 now
where the time goes in v5:
time: 62 us; the launch traced here: 61 us
  Pallas kernels  54.6 us (88%)
  local copies, waits for them, and re-layouts  4.41 us (7%)
  between operations  1.94 us (3%)
    pallas_call x1, Pallas kernels, body(): pl.pallas_call(functools.partial(kernel, n_blk, n_grp, nc), out_shape=(ou...  54.6 us
    unnamed x7, local copies, waits for them, and re-layouts  4.41 us

profile of v5, /device:TPU:1, one launch (start us, length us, event | category | flops | bytes accessed | tf_op | source)
XLA Modules:
  0.0 61.0 jit_solution(255753643259959385)
XLA Ops:
  1.9 0.0 copy-start
  1.9 1.0 %copy-done = bf16[192,1152]{1,0:T(8,128)(2,1)S(1)} copy-done((bf16[192,1152]{1,0:T(8,128)(2,1)S(1)}, bf16[192,1152]{1,0:T(8,128)(2,1)}, u32[]{:S(2)}) %copy-start) | copy-done | bytes 442392
  2.9 0.0 copy-start.1
  2.9 1.0 %copy-done.1 = bf16[192,1152]{1,0:T(8,128)(2,1)S(1)} copy-done((bf16[192,1152]{1,0:T(8,128)(2,1)S(1)}, bf16[192,1152]{1,0:T(8,128)(2,1)}, u32[]{:S(2)}) %copy-start.1) | copy-done | bytes 442392
  4.0 54.6 %band_loss.1 = (f32[192,1152]{1,0:T(8,128)S(1)}, f32[192,1152]{1,0:T(8,128)S(1)}, f32[1,192]{1,0:T(1,128)S(1)}) custom-call(bf16[192,1152]{1,0:T(8,128)(2,1)S(1)} %copy-done, bf16[192,1152]{1,0:T(8,128)(2,1)S(1)} %copy-done.1, f32[1]{0:T(128)S(6)} %copy.10.scale_ref, f32[1]{0:T(128)S(6)} %copy.11.bias_ref), custom_call_target="tpu_custom_call" | custom-call | flops 2038431744 | bytes 2654208 | tf_op jit(solution)/shard_map/band_loss/pallas_call | solution.py:448
  58.6 0.9 %copy.12 = f32[192,1152]{1,0:T(8,128)} copy(f32[192,1152]{1,0:T(8,128)S(1)} %get-tuple-element.12) | data formatting | bytes 1769472
  59.5 0.9 %copy.13 = f32[192,1152]{1,0:T(8,128)} copy(f32[192,1152]{1,0:T(8,128)S(1)} %get-tuple-element.13) | data formatting | bytes 1769472
  60.4 0.6 copy.14
Async XLA Ops:
  1.9 1.0 %copy-start = (bf16[192,1152]{1,0:T(8,128)(2,1)S(1)}, bf16[192,1152]{1,0:T(8,128)(2,1)}, u32[]{:S(2)}) copy-start(bf16[192,1152]{1,0:T(8,128)(2,1)} %img_ref.1) | copy-start | bytes 1327108
  2.9 1.0 %copy-start.1 = (bf16[192,1152]{1,0:T(8,128)(2,1)S(1)}, bf16[192,1152]{1,0:T(8,128)(2,1)}, u32[]{:S(2)}) copy-start(bf16[192,1152]{1,0:T(8,128)(2,1)} %txt_ref.1) | copy-start | bytes 1327108
